TPU v7x, 512 devices: a whole 4x4x16 slice. The times are simulated.
512 devices in a mesh: freq: 8 (over y, core), fibre: 64 (over z, x).
Axes of the slice: x: 4, y: 4, z: 16, core: 2. Of those that a mesh axis runs over, the one named last changes fastest.
Arguments:
- spectra: bfloat16 [16, 2, 512, 32768], P('freq', None, None, 'fibre')
- pairs: int32 [256, 4], P('fibre'), may hold values from 0 to 255, as said below
- refs: int32 [2], replicated, may hold values from 0 to 255
Outputs:
- pair_grams: bfloat16 [16, 256, 4, 2, 128, 128], P('freq', 'fibre')
- ref_grams: bfloat16 [16, 256, 2, 2, 128, 128], P('freq', 'fibre')
Inputs may be any that keep to these rules, and one draw needn't show every extreme that they name: `pairs`: each row lists 4 different blocks other than its own, none more than 4 blocks away from it; the first and the last block are partners of some row.
All inputs are finite; a program needn't handle non-finite values.
Results may differ from a plain program's by a relative error of at most 0.0057.
Values may be sent and summed in bfloat16 or wider, within the bound.
A program may use at most 64 MiB of HBM per device.

v0:
```python
import math

import jax
import jax.numpy as jnp
from jax import lax
from jax.sharding import PartitionSpec as P

BLK = 128
NP = 4
REACH = 4


EPS = 1e-06


def extended_2(shard, sides, width):
    for axis, dim in sides:
        size, length = (lax.axis_size(axis), shard.shape[dim])
        up = [(i, (i + 1) % size) for i in range(size - 1)]
        down = [(j, i) for i, j in up]
        last = lax.slice_in_dim(shard, length - width, length, axis=dim)
        initial = lax.slice_in_dim(shard, 0, width, axis=dim)
        before = lax.ppermute(last, axis, up)
        after = lax.ppermute(initial, axis, down)
        shard = jnp.concatenate([before, shard, after], axis=dim)
    return shard


def from_root(shard, axis, root):
    mine = lax.axis_index(axis) == root
    return lax.psum(jnp.where(mine, shard, jnp.zeros_like(shard)), axis)


def split_parts(block):
    bins, _, segs, width = block.shape
    left = block.reshape(bins, 2 * segs, width)
    rotated = jnp.concatenate([block[:, 1], -block[:, 0]], axis=1)
    return (left, rotated)


def cross_pair(left, right, rotated, scale):
    real = jnp.einsum("fsi,fsj->fij", left, right, preferred_element_type=jnp.float32)
    imag = jnp.einsum("fsi,fsj->fij", left, rotated, preferred_element_type=jnp.float32)
    return (jnp.stack([real, imag], 1) * scale).astype(jnp.bfloat16)


def body(spectra, pairs, refs):
    bins, _, segs, chan = spectra.shape
    nblk = chan // BLK
    widened = spectra.astype(jnp.float32)
    power = jnp.sum(widened * widened, axis=(1, 2)) / segs
    total_bins = bins * lax.axis_size("freq")
    first_bin = lax.axis_index("freq") * bins
    bin_index = first_bin + jnp.arange(bins)
    extended_power = extended_2(power, (("freq", 0),), 1)
    summed = extended_power[:-2] + extended_power[1:-1] + extended_power[2:]
    count = (
        3.0
        - (bin_index == 0).astype(jnp.float32)
        - (bin_index == total_bins - 1).astype(jnp.float32)
    )
    smooth = summed / count[:, None]
    whitened = (widened / jnp.sqrt(smooth + EPS)[:, None, None, :]).astype(jnp.bfloat16)
    scale = 1.0 / math.sqrt(segs)
    extended = extended_2(whitened, (("fibre", 3),), REACH * BLK)
    base = lax.axis_index("fibre") * nblk
    own_left = []
    partner_left = []
    partner_rotated = []
    for local in range(nblk):
        left, rotated = split_parts(whitened[..., local * BLK : (local + 1) * BLK])
        own_left.append(left)
        row_left = []
        row_rotated = []
        for slot in range(NP):
            start = (pairs[local, slot] - base + REACH) * BLK
            partner = lax.dynamic_slice_in_dim(extended, start, BLK, 3)
            other_left, other_rotated = split_parts(partner)
            row_left.append(other_left)
            row_rotated.append(other_rotated)
        partner_left.append(row_left)
        partner_rotated.append(row_rotated)
    rows = []
    for local in range(nblk):
        row = [
            cross_pair(
                own_left[local], partner_left[local][slot], partner_rotated[local][slot], scale
            )
            for slot in range(NP)
        ]
        rows.append(jnp.stack(row, 1))
    pair_grams = jnp.stack(rows, 1)
    owned = []
    owners = []
    for which in range(2):
        owner = refs[which] // nblk
        local = refs[which] - owner * nblk
        owned.append(lax.dynamic_slice_in_dim(whitened, local * BLK, BLK, 3))
        owners.append(owner)
    ref_blocks = []
    for which in range(2):
        ref_blocks.append(from_root(owned[which], "fibre", owners[which]))
    ref_stack = jnp.stack(ref_blocks, 0)
    ref_left = jnp.stack([split_parts(ref_stack[which])[0] for which in range(2)], 1)
    ref_rotated = jnp.stack([split_parts(ref_stack[which])[1] for which in range(2)], 1)
    left_all = jnp.stack(own_left, 1)
    real = jnp.einsum("fasi,frsj->farij", left_all, ref_left, preferred_element_type=jnp.float32)
    imag = jnp.einsum("fasi,frsj->farij", left_all, ref_rotated, preferred_element_type=jnp.float32)
    ref_grams = (jnp.stack([real, imag], 3) * scale).astype(jnp.bfloat16)
    return (pair_grams, ref_grams)


def solution(mesh):
    return jax.shard_map(
        body,
        mesh=mesh,
        in_specs=(P("freq", None, None, "fibre"), P("fibre", None), P()),
        out_specs=(
            P("freq", "fibre", None, None, None, None),
            P("freq", "fibre", None, None, None, None),
        ),
        check_vma=False,
    )
```

profile of v0, /device:TPU:16, one launch (start us, length us, event | category | flops | bytes accessed | tf_op | source)
XLA Modules:
  0.0 352.8 jit_solution(8080077094377732128)
XLA Ops:
  7.2 2.0 fusion
  9.3 1.9 collective-permute-start
  11.2 3.6 %collective-permute-start.1 = (f32[1,512]{1,0:T(1,128)S(1)}, f32[1,512]{1,0:T(1,128)S(1)}, u32[]{:S(2)}, u32[]{:S(2)}) collective-permute-start(f32[1,512]{1,0:T(1,128)S(1)} %get-tuple-element.67), channel_id=1, source_target_pairs={{64,0},{128,64},{192,128},{256,192},{320,256},{384,320},{448,384},... | collective-permute-start | bytes 6152 | tf_op jit(solution)/shard_map/ppermute | solution.py:24
  14.9 0.6 fusion.113
  22.1 2.1 fusion.1
  24.2 1.8 dynamic-slice_select_fusion.1
  26.1 1.3 collective-permute-start.3
  27.4 5.9 %collective-permute-start.2 = (bf16[2,2,512,512]{3,2,0,1:T(8,128)(2,1)S(1)}, bf16[2,2,512,512]{3,2,0,1:T(8,128)(2,1)}, u32[]{:S(2)}, u32[]{:S(2)}) collective-permute-start(bf16[2,2,512,512]{3,2,0,1:T(8,128)(2,1)S(1)} %fusion.1), channel_id=1, source_target_pairs={{0,1},{1,2},{2,3},{3,4},{4,5},{5,6},{6,7},{7,8},{8,9},{9,10},{10,1... | collective-permute-start | bytes 6291464 | tf_op jit(solution)/shard_map/ppermute | solution.py:23
  33.3 0.7 fusion.112
  44.0 0.8 copy.60
  44.8 1.1 copy.12
  45.9 1.9 copy.43
  47.8 0.8 copy.30
  48.7 1.1 copy.17
  49.7 1.4 reshape.637
  51.2 254.5 %all-reduce.3.cloned.1.call-done = (bf16[2,2,512,128]{3,2,0,1:T(8,128)(2,1)}, bf16[2,2,512,128]{3,2,0,1:T(8,128)(2,1)}) async-done(((bf16[2,2,512,128]{3,2,0,1:T(8,128)(2,1)}, bf16[2,2,512,128]{3,2,0,1:T(8,128)(2,1)}), (bf16[2,2,512,128]{3,2,0,1:T(8,128)(2,1)}, bf16[2,2,512,128]{3,2,0,1:T(8,128)(2,1)})) %all-reduce.3.cloned.1.call-update) | async-done | bytes 1048592 | tf_op jit(solution)/shard_map/psum | solution.py:31
  305.6 1.9 copy.57
  307.5 2.0 copy.59
  309.5 1.9 copy.56
  311.4 2.0 copy.58
  313.5 1.4 slice_bitcast_fusion
  315.4 0.9 convolution_bitcast_fusion.1
  316.3 1.0 convolution_bitcast_fusion
  317.4 1.3 fusion.2
  318.6 2.3 copy.70
  320.9 3.3 pad_maximum_fusion
  324.2 1.8 constant_dynamic-slice_fusion.15
  326.0 3.4 dynamic-slice_bitcast_fusion.15
  329.5 0.9 copy-done.3
  330.8 0.4 convolution_bitcast_fusion.5
  331.6 0.4 convolution_bitcast_fusion.9
  332.1 0.5 copy-done.1
  333.4 0.4 convolution_bitcast_fusion.15
  333.8 0.4 convolution_bitcast_fusion.17
  334.6 0.4 convolution_bitcast_fusion.21
  335.0 0.4 convolution_bitcast_fusion.23
  335.4 0.4 convolution_bitcast_fusion.25
  338.2 0.4 convolution_bitcast_fusion.4
  339.0 0.4 convolution_bitcast_fusion.8
  339.3 0.4 convolution_bitcast_fusion.10
  339.7 0.6 convolution_bitcast_fusion.12
  340.3 0.4 convolution_bitcast_fusion.14
  340.6 0.4 convolution_bitcast_fusion.16
  341.0 0.4 convolution_bitcast_fusion.18
  341.4 0.4 convolution_bitcast_fusion.20
  341.7 0.4 convolution_bitcast_fusion.22
  342.1 0.4 convolution_bitcast_fusion.24
  344.5 1.5 copy.69
  (86 shorter events, 7.6 us)
Async XLA Ops:
  7.2 7.7 %copy-start.15 = (s32[2]{0:T(128)S(1)}, s32[2]{0:T(128)}, u32[]{:S(2)}) copy-start(s32[2]{0:T(128)} %param.5) | copy-start | bytes 28
  7.2 298.4 %all-reduce.3.cloned.1.call-start = ((), (), s32[]{:S(2)}) async-start(), calls=%async_computation | async-start | bytes 2097152 | tf_op jit(solution)/shard_map/psum | solution.py:31
  9.3 12.7 %collective-permute-start = (f32[1,512]{1,0:T(1,128)S(1)}, f32[1,512]{1,0:T(1,128)S(1)}, u32[]{:S(2)}, u32[]{:S(2)}) collective-permute-start(f32[1,512]{1,0:T(1,128)S(1)} %get-tuple-element.66), channel_id=1, source_target_pairs={{0,64},{64,128},{128,192},{192,256},{256,320},{320,384},{384,448},... | collective-permute-start | bytes 6152 | tf_op jit(solution)/shard_map/ppermute | solution.py:23
  11.2 10.8 %collective-permute-start.1 = (f32[1,512]{1,0:T(1,128)S(1)}, f32[1,512]{1,0:T(1,128)S(1)}, u32[]{:S(2)}, u32[]{:S(2)}) collective-permute-start(f32[1,512]{1,0:T(1,128)S(1)} %get-tuple-element.67), channel_id=1, source_target_pairs={{64,0},{128,64},{192,128},{256,192},{320,256},{384,320},{448,384},... | collective-permute-start | bytes 6152 | tf_op jit(solution)/shard_map/ppermute | solution.py:24
  24.2 9.1 %copy-start.14 = (s32[4,4]{1,0:T(4,128)S(1)}, s32[4,4]{1,0:T(4,128)}, u32[]{:S(2)}) copy-start(s32[4,4]{1,0:T(4,128)} %param.4) | copy-start | bytes 196
  26.1 294.8 %collective-permute-start.3 = (bf16[2,2,512,512]{3,2,0,1:T(8,128)(2,1)S(1)}, bf16[2,2,512,512]{3,2,0,1:T(8,128)(2,1)}, u32[]{:S(2)}, u32[]{:S(2)}) collective-permute-start(bf16[2,2,512,512]{3,2,0,1:T(8,128)(2,1)S(1)} %fusion.1), channel_id=1, source_target_pairs={{1,0},{2,1},{3,2},{4,3},{5,4},{6,5},{7,6},{8,7},{9,8},{10,9},{11,1... | collective-permute-start | bytes 6291464 | tf_op jit(solution)/shard_map/ppermute | solution.py:24
  27.4 293.5 %collective-permute-start.2 = (bf16[2,2,512,512]{3,2,0,1:T(8,128)(2,1)S(1)}, bf16[2,2,512,512]{3,2,0,1:T(8,128)(2,1)}, u32[]{:S(2)}, u32[]{:S(2)}) collective-permute-start(bf16[2,2,512,512]{3,2,0,1:T(8,128)(2,1)S(1)} %fusion.1), channel_id=1, source_target_pairs={{0,1},{1,2},{2,3},{3,4},{4,5},{5,6},{6,7},{7,8},{8,9},{9,10},{10,1... | collective-permute-start | bytes 6291464 | tf_op jit(solution)/shard_map/ppermute | solution.py:23
  313.4 1.6 copy-start
  313.4 1.6 copy-start.2
  313.4 1.7 copy-start.4
  313.4 1.8 copy-start.5
  313.4 2.0 copy-start.6
  329.4 1.0 copy-start.3
  331.6 1.0 copy-start.1
  336.4 1.0 copy-start.12
  336.4 1.0 copy-start.13
  336.8 1.0 copy-start.10
  336.8 1.1 copy-start.11
  336.8 1.4 copy-start.8
  336.9 1.4 copy-start.9
  337.2 1.4 copy-start.7
Sparse Core Ops, SparseCore 0:
  26.2 279.3 all-reduce.2
where the time goes:
time: 354 us; the launch traced here: 353 us
  waiting for transfers between devices  254 us (72%)
  between operations  31.2 us (9%)
  local copies, waits for them, and re-layouts  24.7 us (7%)
  other arithmetic  16.7 us (5%)
  matrix products  13 us (4%)
  starting transfers between devices  12.8 us (4%)
    psum x1, waiting for transfers between devices, from_root(): return lax.psum(jnp.where(mine, shard, jnp.zeros_like(shard)), axis)  254 us
    ppermute x2, starting transfers between devices, extended_2(): before = lax.ppermute(last, axis, up)  7.81 us
  transfers between devices with their start and end apart: 5, of which 1 were waited for; matrix products, arithmetic and copies ran while one was open for 7% of the time, Pallas kernels for 0%

commit v1 on v0

v1 whole, which is shorter than its diff:
```python
import math

import jax
import jax.numpy as jnp
from jax import lax
from jax.experimental import pallas as pl
from jax.experimental.pallas import tpu as pltpu
from jax.sharding import PartitionSpec as P

BLK = 128
NP = 4
SEGS = 512
EPS = 1e-06
BINS = 2
NBLK = 4
CHAN = NBLK * BLK
PAIR = 2 * BLK
NX = 4
NZ = 16
NF = 8
NFIB = NX * NZ
SCALE = 1.0 / math.sqrt(SEGS)
MESH = pl.DeviceIdType.MESH
TO_RIGHT = ((0, 0), (1, 0), (1, 1))
TO_LEFT = ((2, 2), (3, 2), (3, 3))
SLOTS = 14
LEFT, OWN0, OWN1, RIGHT, REFS = range(5)


def kernel(
    refs_ref, spec_hbm, g_hbm,
    raw, white, lhs, halo, mine, ring, xsend, xrecv, full, stage, gsend, grecv,
    psend, precv, inv_own, inv_halo, mask_ref,
    load_sem, pow_s, pow_r, halo_s, halo_r, ring_s, ring_r, x_s, x_r, ag_s, ag_r,
    gs_s, gs_r, inv_s, inv_r, out_sem, far_sem,
):
    f32, bf = jnp.float32, jnp.bfloat16
    fq = lax.axis_index("freq")
    fb = lax.axis_index("fibre")
    x = lax.rem(fb, NX)
    z = fb // NX
    f_up, f_dn = lax.rem(fq + 1, NF), lax.rem(fq + NF - 1, NF)
    right, left = lax.rem(fb + 1, NFIB), lax.rem(fb + NFIB - 1, NFIB)
    z_up, z_dn = lax.rem(fb + NX, NFIB), lax.rem(fb + NFIB - NX, NFIB)
    peers = [z * NX + lax.rem(x + o, NX) for o in (1, 2, 3)]

    def remote(src, dst, s_sem, r_sem, f, d):
        return pltpu.make_async_remote_copy(
            src, dst, s_sem, r_sem, device_id=(f, d), device_id_type=MESH)

    loads = [
        pltpu.make_async_copy(
            spec_hbm.at[b, :, :, pl.ds(h * PAIR, PAIR)], raw.at[h, b], load_sem.at[b, h])
        for b in range(BINS) for h in range(2)
    ]
    for c in loads:
        c.start()

    barrier = pltpu.get_barrier_semaphore()
    for f in (f_up, f_dn):
        pl.semaphore_signal(barrier, inc=1, device_id=(f, fb), device_id_type=MESH)
    for d in [right, left, z_up, z_dn] + peers:
        pl.semaphore_signal(barrier, inc=1, device_id=(fq, d), device_id_type=MESH)

    block = fb * NBLK + lax.broadcasted_iota(jnp.int32, (16, CHAN), 1) // BLK
    for r in range(2):
        mask_ref[r] = jnp.where(block == refs_ref[r], 1.0, 0.0).astype(bf)

    def gather_lanes(t):
        return (t[..., :BLK] + t[..., BLK:2 * BLK]) + (t[..., 2 * BLK:3 * BLK] + t[..., 3 * BLK:])

    def gather_two(t):
        return t[..., :BLK] + t[..., BLK:]

    for b in range(BINS):
        loads[2 * b].wait()
        loads[2 * b + 1].wait()

        def pick(i, _, b=b):
            for part in range(2):
                v = [raw[h, b, part, pl.ds(i * 128, 128), :].reshape(8, 16, PAIR) for h in range(2)]
                for r in range(2):
                    m = mask_ref[r]
                    t = gather_two(v[0] * m[None, :, :PAIR]) + gather_two(v[1] * m[None, :, PAIR:])
                    mine[b * 8 + part * 4 + i, :, r * BLK:(r + 1) * BLK] = t.reshape(128, BLK)
            return 0

        lax.fori_loop(0, 4, pick, 0)

    def ring_copy(way, s, k):
        rows = pl.ds(k * 64, 64)
        src = mine.at[lax.rem(z + 8, NZ) if way == 0 else lax.rem(z + NZ - 7, NZ), rows]
        if not (isinstance(s, int) and s == 0):
            src = ring.at[way, s, rows]
        return remote(src, ring.at[way, s + 1, rows], ring_s.at[way, s, k], ring_r.at[way, s, k],
                      fq, z_up if way == 0 else z_dn)

    def halo_copy(b, side, part):
        return remote(raw.at[1 - side, b, part], halo.at[side, b, part], halo_s.at[side, b, part],
                      halo_r.at[side, b, part], fq, right if side == 0 else left)

    def inv_copy(side):
        cols = pl.ds(2 * BLK, 2 * BLK) if side == 0 else pl.ds(0, 2 * BLK)
        return remote(inv_own.at[:, :, cols], inv_halo.at[side], inv_s.at[side], inv_r.at[side],
                      fq, right if side == 0 else left)

    pl.semaphore_wait(barrier, 9)
    for k in range(2):
        for way in range(2):
            ring_copy(way, 0, k).start()

    def halo_start(b, part):
        for side in range(2):
            halo_copy(b, side, part).start()

    halo_start(0, 0)

    def reduce_step(s):
        for k in range(2):
            rows = pl.ds(k * 64, 64)
            ring_copy(0, s, k).wait_recv()
            ring[0, s + 1, rows] = ring[0, s + 1, rows] + mine[lax.rem(z + 7 - s + NZ, NZ), rows]
            if s < 7:
                ring_copy(0, s + 1, k).start()
            if s < 7:
                ring_copy(1, s, k).wait_recv()
            if s < 6:
                ring[1, s + 1, rows] = ring[1, s + 1, rows] + mine[lax.rem(z + NZ - 6 + s, NZ), rows]
                ring_copy(1, s + 1, k).start()

    for b in range(BINS):
        def add(i, acc, b=b):
            for part in range(2):
                v = [raw[h, b, part, pl.ds(i * 64, 64), :].astype(f32) for h in range(2)]
                acc = [a + jnp.sum((w * w).reshape(8, 8, PAIR), axis=0) for a, w in zip(acc, v)]
            return acc

        acc = lax.fori_loop(0, SEGS // 64, add, [jnp.zeros((8, PAIR), f32)] * 2)
        psend[b, :, :PAIR] = acc[0]
        psend[b, :, PAIR:] = acc[1]

    up = remote(psend.at[1], precv.at[0], pow_s.at[0], pow_r.at[0], f_up, fb)
    dn = remote(psend.at[0], precv.at[1], pow_s.at[1], pow_r.at[1], f_dn, fb)
    up.start()
    dn.start()
    reduce_step(0)

    def total(v):
        return jnp.sum(v, axis=0, keepdims=True) / SEGS

    p0, p1 = total(psend[0]), total(psend[1])
    up.wait()
    dn.wait()
    below = jnp.where(fq == 0, 0.0, total(precv[0]))
    above = jnp.where(fq == NF - 1, 0.0, total(precv[1]))
    c0 = jnp.where(fq == 0, 2.0, 3.0)
    c1 = jnp.where(fq == NF - 1, 2.0, 3.0)
    smooth = [(below + p0 + p1) / c0, (p0 + p1 + above) / c1]
    row = lax.broadcasted_iota(jnp.int32, (16, BLK), 0)
    for b in range(BINS):
        inv_own[b] = jnp.broadcast_to(1.0 / jnp.sqrt(smooth[b] + EPS), (8, CHAN))
    inv_copy(0).start()
    inv_copy(1).start()
    for r in range(2):
        tile = jnp.zeros((16, BLK), f32)
        for b in range(BINS):
            v = gather_lanes(inv_own[b, 0:1, :] * mask_ref[r, 0:1, :].astype(f32))
            for piece in range(3):
                part = v.astype(bf).astype(f32)
                tile = jnp.where(row == b * 3 + piece, jnp.broadcast_to(part, (16, BLK)), tile)
                v = v - part
        xsend[128:144, r * BLK:(r + 1) * BLK] = tile.astype(bf)
    reduce_step(1)
    halo_start(0, 1)

    def whiten(b):
        def turn(i, _):
            rows = pl.ds(pl.multiple_of(i * 128, 128), 128)
            rows2 = pl.ds(pl.multiple_of(SEGS + i * 128, 128), 128)
            for h in range(2):
                cols = slice(h * PAIR, (h + 1) * PAIR)
                inv = inv_own[b, 0:1, cols]
                re = (raw[h, b, 0, rows, :].astype(f32) * inv).astype(bf)
                im = (raw[h, b, 1, rows, :].astype(f32) * inv).astype(bf)
                white[h, b, 0, rows, :] = re
                white[h, b, 1, rows, :] = im
                re, im = re.T, im.T
                lhs[b, 0, cols, rows] = re
                lhs[b, 0, cols, rows2] = im
                lhs[b, 1, cols, rows] = -im
                lhs[b, 1, cols, rows2] = re
            return 0

        lax.fori_loop(0, SEGS // 128, turn, 0)

    def half_gram(b, group, part, rhs):
        res = jnp.dot(lhs[b, part], rhs, preferred_element_type=f32) * SCALE
        res = res.astype(bf)
        for q in range(2):
            for a in range(NBLK):
                stage[b, group, q, a, part] = res[a * BLK:(a + 1) * BLK, q * BLK:(q + 1) * BLK]

    def out_copy(b, group):
        return pltpu.make_async_copy(
            stage.at[b, group], g_hbm.at[pl.ds(2 + 2 * group, 2), b], out_sem.at[b, group])

    def own_grams(b, pair):
        def part_of(part, _):
            half_gram(b, OWN0 + pair, part, white[pair, b].reshape(2 * SEGS, 2 * BLK))
            return 0

        lax.fori_loop(0, 2, part_of, 0)
        out_copy(b, OWN0 + pair).start()

    whiten(0)
    reduce_step(2)
    whiten(1)
    reduce_step(3)
    halo_start(1, 0)
    own_grams(0, 0)
    reduce_step(4)
    own_grams(0, 1)
    reduce_step(5)
    halo_start(1, 1)
    own_grams(1, 0)
    reduce_step(6)
    own_grams(1, 1)
    for k in range(2):
        ring_copy(0, 7, k).wait_recv()
    xsend[0:128] = mine[z] + ring[0, 8] + ring[1, 7]

    x_copies = [
        remote(xsend, xrecv.at[o], x_s.at[o], x_r.at[o], fq, peers[o]) for o in range(3)
    ]
    for c in x_copies:
        c.start()

    def gram_copy(b, side, n):
        return remote(gsend.at[b, side, n], grecv.at[b, side, n], gs_s.at[b, side, n],
                      gs_r.at[b, side, n], fq, right if side == 0 else left)

    def halo_grams(b):
        for side, group in ((0, LEFT), (1, RIGHT)):
            for part in range(2):
                halo_copy(b, side, part).wait_recv()

            def scale(i, _, side=side):
                rows = pl.ds(i * 64, 64)
                for part in range(2):
                    v = halo[side, b, part, rows, :].astype(f32) * inv_halo[side, b, 0:1, :]
                    halo[side, b, part, rows, :] = v.astype(bf)
                return 0

            lax.fori_loop(0, SEGS // 64, scale, 0)

            def part_of(part, _, side=side, group=group):
                half_gram(b, group, part, halo[side, b].reshape(2 * SEGS, 2 * BLK))
                return 0

            lax.fori_loop(0, 2, part_of, 0)
            out_copy(b, group).start()
            if side == 1:
                for n, (la, lb) in enumerate(TO_RIGHT):
                    gsend[b, 0, n, 0] = stage[b, RIGHT, lb, la, 0].T
                    gsend[b, 0, n, 1] = -stage[b, RIGHT, lb, la, 1].T
                    gram_copy(b, 0, n).start()
            else:
                for n, (la, lb) in enumerate(TO_LEFT):
                    gsend[b, 1, n, 0] = stage[b, LEFT, la - 2, lb, 0].T
                    gsend[b, 1, n, 1] = -stage[b, LEFT, la - 2, lb, 1].T
                    gram_copy(b, 1, n).start()

    inv_copy(0).wait_recv()
    inv_copy(1).wait_recv()
    halo_grams(0)

    for c in x_copies:
        c.wait_recv()
    full[z] = xsend[...] + xrecv[0] + xrecv[1] + xrecv[2]

    def ag_copy(way, s, k):
        rows = pl.ds(0, 64) if k == 0 else pl.ds(64, 80)
        c = lax.rem(z + NZ - s, NZ) if way == 0 else lax.rem(z + s, NZ)
        return remote(full.at[c, rows], full.at[c, rows], ag_s.at[way, s, k], ag_r.at[way, s, k],
                      fq, z_up if way == 0 else z_dn)

    for k in range(2):
        for way in range(2):
            ag_copy(way, 0, k).start()

    def gather_step(s, _):
        for k in range(2):
            ag_copy(0, s, k).wait_recv()

            @pl.when(s < 7)
            def _():
                ag_copy(0, s + 1, k).start()
                ag_copy(1, s, k).wait_recv()

            @pl.when(s < 6)
            def _():
                ag_copy(1, s + 1, k).start()
        return 0

    lax.fori_loop(0, 2, gather_step, 0)
    halo_grams(1)
    lax.fori_loop(2, 8, gather_step, 0)

    for s in range(8):
        for k in range(2):
            ring_copy(0, s, k).wait_send()
            if s < 7:
                ring_copy(1, s, k).wait_send()
    for b in range(BINS):
        for side in range(2):
            for part in range(2):
                halo_copy(b, side, part).wait_send()

    tail = full[0, 128:144, :].astype(f32)
    for c in range(1, NZ):
        tail = tail + full[c, 128:144, :].astype(f32)
    for b in range(BINS):
        inv = tail[b * 3:b * 3 + 1] + tail[b * 3 + 1:b * 3 + 2] + tail[b * 3 + 2:b * 3 + 3]

        def scale(i, _, b=b, inv=inv):
            c = b * 8 + i // 2
            rows = pl.ds(pl.multiple_of(lax.rem(i, 2) * 64, 64), 64)
            mine[c, rows, :] = (full[c, rows, :].astype(f32) * inv).astype(bf)
            return 0

        lax.fori_loop(0, 16, scale, 0)

        def part_of(part, _, b=b):
            half_gram(b, REFS, part, mine[b * 8:b * 8 + 8].reshape(2 * SEGS, 2 * BLK))
            return 0

        lax.fori_loop(0, 2, part_of, 0)
        out_copy(b, REFS).start()

    def far_copy(b, side, n):
        if side == 0:
            la, lb = TO_RIGHT[n]
            slot, a = la, lb
        else:
            la, lb = TO_LEFT[n]
            slot, a = 10 + lb, la
        return pltpu.make_async_copy(
            grecv.at[b, side, n], g_hbm.at[slot, b, a], far_sem.at[b, side, n])

    for b in range(BINS):
        for side in range(2):
            for n in range(3):
                gram_copy(b, side, n).wait_recv()
                far_copy(b, side, n).start()

    for b in range(BINS):
        for side in range(2):
            for n in range(3):
                gram_copy(b, side, n).wait_send()
                far_copy(b, side, n).wait()
        for group in range(5):
            out_copy(b, group).wait()
    for c in x_copies:
        c.wait_send()
    for side in range(2):
        inv_copy(side).wait_send()

    def drain(s, _):
        for k in range(2):
            ag_copy(0, s, k).wait_send()

            @pl.when(s < 7)
            def _():
                ag_copy(1, s, k).wait_send()
        return 0

    lax.fori_loop(0, 8, drain, 0)


def select_kernel(pairs_ref, g_hbm, pair_out, ref_out, pair_buf, ref_buf, pair_sem, ref_sem):
    base = lax.axis_index("fibre") * NBLK
    copies = []
    for a in range(NBLK):
        for p in range(NP):
            e = pairs_ref[a, p] - base + NBLK
            slot = jnp.where(e >= 10, e + 2, e)
            copies.append((
                pltpu.make_async_copy(g_hbm.at[slot, :, a], pair_buf.at[a, p], pair_sem.at[0, a, p]),
                pltpu.make_async_copy(pair_buf.at[a, p], pair_out.at[:, a, p], pair_sem.at[1, a, p])))
    for r in range(2):
        copies.append((
            pltpu.make_async_copy(g_hbm.at[10 + r], ref_buf.at[r], ref_sem.at[0, r]),
            pltpu.make_async_copy(ref_buf.at[r], ref_out.at[:, :, r], ref_sem.at[1, r])))
    for c, _ in copies:
        c.start()
    for c, d in copies:
        c.wait()
        d.start()
    for _, d in copies:
        d.wait()


def body(spectra, pairs, refs):
    bf = jnp.bfloat16
    smem = pl.BlockSpec(memory_space=pltpu.SMEM)
    hbm = pl.BlockSpec(memory_space=pl.ANY)
    dma = pltpu.SemaphoreType.DMA
    grams = pl.pallas_call(
        kernel,
        out_shape=jax.ShapeDtypeStruct((SLOTS, BINS, NBLK, 2, BLK, BLK), bf),
        in_specs=[smem, hbm],
        out_specs=hbm,
        scratch_shapes=[
            pltpu.VMEM((2, BINS, 2, SEGS, PAIR), bf),
            pltpu.VMEM((2, BINS, 2, SEGS, PAIR), bf),
            pltpu.VMEM((BINS, 2, CHAN, 2 * SEGS), bf),
            pltpu.VMEM((2, BINS, 2, SEGS, 2 * BLK), bf),
            pltpu.VMEM((NZ, 128, 2 * BLK), bf),
            pltpu.VMEM((2, 9, 128, 2 * BLK), bf),
            pltpu.VMEM((144, 2 * BLK), bf),
            pltpu.VMEM((3, 144, 2 * BLK), bf),
            pltpu.VMEM((NZ, 144, 2 * BLK), bf),
            pltpu.VMEM((BINS, 5, 2, NBLK, 2, BLK, BLK), bf),
            pltpu.VMEM((BINS, 2, 3, 2, BLK, BLK), bf),
            pltpu.VMEM((BINS, 2, 3, 2, BLK, BLK), bf),
            pltpu.VMEM((BINS, 8, CHAN), jnp.float32),
            pltpu.VMEM((2, 8, CHAN), jnp.float32),
            pltpu.VMEM((BINS, 8, CHAN), jnp.float32),
            pltpu.VMEM((2, BINS, 8, 2 * BLK), jnp.float32),
            pltpu.VMEM((2, 16, CHAN), bf),
            dma((BINS, 2)),
            dma((2,)), dma((2,)),
            dma((2, BINS, 2)), dma((2, BINS, 2)),
            dma((2, 8, 2)), dma((2, 8, 2)),
            dma((3,)), dma((3,)),
            dma((2, 8, 2)), dma((2, 8, 2)),
            dma((BINS, 2, 3)), dma((BINS, 2, 3)),
            dma((2,)), dma((2,)),
            dma((BINS, 5)),
            dma((BINS, 2, 3)),
        ],
        compiler_params=pltpu.CompilerParams(
            collective_id=0, has_side_effects=True, vmem_limit_bytes=60 * 1024 * 1024),
        cost_estimate=pl.CostEstimate(
            flops=5_400_000_000, bytes_accessed=8 * 1024 * 1024, transcendentals=1024),
        name="grams",
    )(refs, spectra)
    return pl.pallas_call(
        select_kernel,
        out_shape=(
            jax.ShapeDtypeStruct((BINS, NBLK, NP, 2, BLK, BLK), bf),
            jax.ShapeDtypeStruct((BINS, NBLK, 2, 2, BLK, BLK), bf),
        ),
        in_specs=[smem, hbm],
        out_specs=(hbm, hbm),
        scratch_shapes=[
            pltpu.VMEM((NBLK, NP, BINS, 2, BLK, BLK), bf),
            pltpu.VMEM((2, BINS, NBLK, 2, BLK, BLK), bf),
            dma((2, NBLK, NP)), dma((2, 2)),
        ],
        compiler_params=pltpu.CompilerParams(vmem_limit_bytes=60 * 1024 * 1024),
        cost_estimate=pl.CostEstimate(
            flops=0, bytes_accessed=6 * 1024 * 1024, transcendentals=0),
        name="select",
    )(pairs, grams)


def solution(mesh):
    return jax.shard_map(
        body,
        mesh=mesh,
        in_specs=(P("freq", None, None, "fibre"), P("fibre", None), P()),
        out_specs=(
            P("freq", "fibre", None, None, None, None),
            P("freq", "fibre", None, None, None, None),
        ),
        check_vma=False,
    )
```

time: 354 us -> 95.6 us (0.27)
  the two profiles are of different devices: /device:TPU:16 before, /device:TPU:14 now
where the time goes in v1:
time: 95.6 us; the launch traced here: 95.4 us
  Pallas kernels  94.8 us (99%)
    pallas_call x1, Pallas kernels, body(): pl.pallas_call(kernel, out_shape=jax.ShapeDtypeStruct((SLOTS, BINS, NBLK,...  90.8 us
    pallas_call x1, Pallas kernels, body(): pl.pallas_call(select_kernel, out_shape=(jax.ShapeDtypeStruct((BINS, NBLK...  4.04 us

profile of v1, /device:TPU:14, one launch (start us, length us, event | category | flops | bytes accessed | tf_op | source)
XLA Modules:
  0.0 95.4 jit_solution(12217181820445324231)
XLA Ops:
  0.6 90.8 %grams.1.g_hbm = bf16[14,2,4,2,128,128]{5,4,3,2,1,0:T(8,128)(2,1)} custom-call(s32[2]{0:T(128)} %refs_ref.1, bf16[2,2,512,512]{3,2,1,0:T(8,128)(2,1)} %spec_hbm.1), custom_call_target="tpu_custom_call" | custom-call | flops 5400000000 | bytes 8388608 | tf_op jit(solution)/shard_map/grams/pallas_call | solution.py:408
  91.4 4.0 %select.1 = (bf16[2,4,4,2,128,128]{5,4,3,2,1,0:T(8,128)(2,1)}, bf16[2,4,2,2,128,128]{5,4,3,2,1,0:T(8,128)(2,1)}) custom-call(s32[4,4]{1,0:T(4,128)} %pairs_ref.1, bf16[14,2,4,2,128,128]{5,4,3,2,1,0:T(8,128)(2,1)} %grams.1.g_hbm), custom_call_target="tpu_custom_call" | custom-call | bytes 6291456 | tf_op jit(solution)/shard_map/select/pallas_call | solution.py:448

commit v2 on v1

--- a/solution.py
+++ b/solution.py
@@ -95,9 +95,11 @@
         return remote(src, ring.at[way, s + 1, rows], ring_s.at[way, s, k], ring_r.at[way, s, k],
                       fq, z_up if way == 0 else z_dn)
 
-    def halo_copy(b, side, part):
-        return remote(raw.at[1 - side, b, part], halo.at[side, b, part], halo_s.at[side, b, part],
-                      halo_r.at[side, b, part], fq, right if side == 0 else left)
+    def halo_copy(b, side, part, half):
+        rows = pl.ds(half * 256, 256)
+        return remote(raw.at[1 - side, b, part, rows], halo.at[side, b, part, rows],
+                      halo_s.at[side, b, part, half], halo_r.at[side, b, part, half],
+                      fq, right if side == 0 else left)
 
     def inv_copy(side):
         cols = pl.ds(2 * BLK, 2 * BLK) if side == 0 else pl.ds(0, 2 * BLK)
@@ -109,11 +111,11 @@
         for way in range(2):
             ring_copy(way, 0, k).start()
 
-    def halo_start(b, part):
+    def halo_start(piece):
         for side in range(2):
-            halo_copy(b, side, part).start()
-
-    halo_start(0, 0)
+            halo_copy(piece // 4, side, piece // 2 % 2, piece % 2).start()
+
+    halo_start(0)
 
     def reduce_step(s):
         for k in range(2):
@@ -144,6 +146,7 @@
     up.start()
     dn.start()
     reduce_step(0)
+    halo_start(1)
 
     def total(v):
         return jnp.sum(v, axis=0, keepdims=True) / SEGS
@@ -171,7 +174,7 @@
                 v = v - part
         xsend[128:144, r * BLK:(r + 1) * BLK] = tile.astype(bf)
     reduce_step(1)
-    halo_start(0, 1)
+    halo_start(2)
 
     def whiten(b):
         def turn(i, _):
@@ -214,14 +217,16 @@
 
     whiten(0)
     reduce_step(2)
+    halo_start(3)
     whiten(1)
     reduce_step(3)
-    halo_start(1, 0)
+    halo_start(4)
     own_grams(0, 0)
     reduce_step(4)
+    halo_start(5)
     own_grams(0, 1)
     reduce_step(5)
-    halo_start(1, 1)
+    halo_start(6)
     own_grams(1, 0)
     reduce_step(6)
     own_grams(1, 1)
@@ -234,6 +239,7 @@
     ]
     for c in x_copies:
         c.start()
+    halo_start(7)
 
     def gram_copy(b, side, n):
         return remote(gsend.at[b, side, n], grecv.at[b, side, n], gs_s.at[b, side, n],
@@ -242,7 +248,8 @@
     def halo_grams(b):
         for side, group in ((0, LEFT), (1, RIGHT)):
             for part in range(2):
-                halo_copy(b, side, part).wait_recv()
+                for half in range(2):
+                    halo_copy(b, side, part, half).wait_recv()
 
             def scale(i, _, side=side):
                 rows = pl.ds(i * 64, 64)
@@ -263,12 +270,10 @@
                 for n, (la, lb) in enumerate(TO_RIGHT):
                     gsend[b, 0, n, 0] = stage[b, RIGHT, lb, la, 0].T
                     gsend[b, 0, n, 1] = -stage[b, RIGHT, lb, la, 1].T
-                    gram_copy(b, 0, n).start()
             else:
                 for n, (la, lb) in enumerate(TO_LEFT):
                     gsend[b, 1, n, 0] = stage[b, LEFT, la - 2, lb, 0].T
                     gsend[b, 1, n, 1] = -stage[b, LEFT, la - 2, lb, 1].T
-                    gram_copy(b, 1, n).start()
 
     inv_copy(0).wait_recv()
     inv_copy(1).wait_recv()
@@ -288,7 +293,7 @@
         for way in range(2):
             ag_copy(way, 0, k).start()
 
-    def gather_step(s, _):
+    def gather_step(s):
         for k in range(2):
             ag_copy(0, s, k).wait_recv()
 
@@ -300,11 +305,24 @@
             @pl.when(s < 6)
             def _():
                 ag_copy(1, s + 1, k).start()
+
+    def gather_and_send(b, first):
+        def step(s, _):
+            gather_step(s)
+            for side in range(2):
+                gram_copy(b, side, s - first).start()
+            return 0
+
+        lax.fori_loop(first, first + 3, step, 0)
+
+    def gather_rest(s, _):
+        gather_step(s)
         return 0
 
-    lax.fori_loop(0, 2, gather_step, 0)
+    gather_and_send(0, 0)
     halo_grams(1)
-    lax.fori_loop(2, 8, gather_step, 0)
+    gather_and_send(1, 3)
+    lax.fori_loop(6, 8, gather_rest, 0)
 
     for s in range(8):
         for k in range(2):
@@ -314,7 +332,8 @@
     for b in range(BINS):
         for side in range(2):
             for part in range(2):
-                halo_copy(b, side, part).wait_send()
+                for half in range(2):
+                    halo_copy(b, side, part, half).wait_send()
 
     tail = full[0, 128:144, :].astype(f32)
     for c in range(1, NZ):
@@ -430,7 +449,7 @@
             pltpu.VMEM((2, 16, CHAN), bf),
             dma((BINS, 2)),
             dma((2,)), dma((2,)),
-            dma((2, BINS, 2)), dma((2, BINS, 2)),
+            dma((2, BINS, 2, 2)), dma((2, BINS, 2, 2)),
             dma((2, 8, 2)), dma((2, 8, 2)),
             dma((3,)), dma((3,)),
             dma((2, 8, 2)), dma((2, 8, 2)),

time: 95.6 us -> 90.3 us (0.945)
  the two profiles are of different devices: /device:TPU:14 before, /device:TPU:8 now
where the time goes in v2:
time: 90.3 us; the launch traced here: 90.1 us
  Pallas kernels  89.5 us (99%)
    pallas_call x1, Pallas kernels, body(): pl.pallas_call(kernel, out_shape=jax.ShapeDtypeStruct((SLOTS, BINS, NBLK,...  85.4 us
    pallas_call x1, Pallas kernels, body(): pl.pallas_call(select_kernel, out_shape=(jax.ShapeDtypeStruct((BINS, NBLK...  4.04 us

profile of v2, /device:TPU:8, one launch (start us, length us, event | category | flops | bytes accessed | tf_op | source)
XLA Modules:
  0.0 90.1 jit_solution(235502271282735948)
XLA Ops:
  0.6 85.4 %grams.1.g_hbm = bf16[14,2,4,2,128,128]{5,4,3,2,1,0:T(8,128)(2,1)} custom-call(s32[2]{0:T(128)} %refs_ref.1, bf16[2,2,512,512]{3,2,1,0:T(8,128)(2,1)} %spec_hbm.1), custom_call_target="tpu_custom_call" | custom-call | flops 5400000000 | bytes 8388608 | tf_op jit(solution)/shard_map/grams/pallas_call | solution.py:427
  86.1 4.0 %select.1 = (bf16[2,4,4,2,128,128]{5,4,3,2,1,0:T(8,128)(2,1)}, bf16[2,4,2,2,128,128]{5,4,3,2,1,0:T(8,128)(2,1)}) custom-call(s32[4,4]{1,0:T(4,128)} %pairs_ref.1, bf16[14,2,4,2,128,128]{5,4,3,2,1,0:T(8,128)(2,1)} %grams.1.g_hbm), custom_call_target="tpu_custom_call" | custom-call | bytes 6291456 | tf_op jit(solution)/shard_map/select/pallas_call | solution.py:467

commit v3 on v2

--- a/solution.py
+++ b/solution.py
@@ -25,6 +25,12 @@
 TO_LEFT = ((2, 2), (3, 2), (3, 3))
 SLOTS = 14
 LEFT, OWN0, OWN1, RIGHT, REFS = range(5)
+PIECES = (
+    (0, 0, 0, 128), (0, 0, 128, 256), (0, 0, 384, 128),
+    (0, 1, 0, 256), (0, 1, 256, 128), (0, 1, 384, 128),
+    (1, 0, 0, 256), (1, 0, 256, 128), (1, 0, 384, 128),
+    (1, 1, 0, 128), (1, 1, 128, 128), (1, 1, 256, 256),
+)
 
 
 def kernel(
@@ -95,11 +101,11 @@
         return remote(src, ring.at[way, s + 1, rows], ring_s.at[way, s, k], ring_r.at[way, s, k],
                       fq, z_up if way == 0 else z_dn)
 
-    def halo_copy(b, side, part, half):
-        rows = pl.ds(half * 256, 256)
+    def halo_copy(n, side):
+        b, part, first, size = PIECES[n]
+        rows = pl.ds(first, size)
         return remote(raw.at[1 - side, b, part, rows], halo.at[side, b, part, rows],
-                      halo_s.at[side, b, part, half], halo_r.at[side, b, part, half],
-                      fq, right if side == 0 else left)
+                      halo_s.at[side, n], halo_r.at[side, n], fq, right if side == 0 else left)
 
     def inv_copy(side):
         cols = pl.ds(2 * BLK, 2 * BLK) if side == 0 else pl.ds(0, 2 * BLK)
@@ -113,7 +119,7 @@
 
     def halo_start(piece):
         for side in range(2):
-            halo_copy(piece // 4, side, piece // 2 % 2, piece % 2).start()
+            halo_copy(piece, side).start()
 
     halo_start(0)
 
@@ -229,6 +235,7 @@
     halo_start(6)
     own_grams(1, 0)
     reduce_step(6)
+    halo_start(7)
     own_grams(1, 1)
     for k in range(2):
         ring_copy(0, 7, k).wait_recv()
@@ -239,7 +246,6 @@
     ]
     for c in x_copies:
         c.start()
-    halo_start(7)
 
     def gram_copy(b, side, n):
         return remote(gsend.at[b, side, n], grecv.at[b, side, n], gs_s.at[b, side, n],
@@ -247,9 +253,8 @@
 
     def halo_grams(b):
         for side, group in ((0, LEFT), (1, RIGHT)):
-            for part in range(2):
-                for half in range(2):
-                    halo_copy(b, side, part, half).wait_recv()
+            for n in range(b * 6, b * 6 + 6):
+                halo_copy(n, side).wait_recv()
 
             def scale(i, _, side=side):
                 rows = pl.ds(i * 64, 64)
@@ -315,25 +320,28 @@
 
         lax.fori_loop(first, first + 3, step, 0)
 
-    def gather_rest(s, _):
+    for s in range(2):
         gather_step(s)
-        return 0
-
-    gather_and_send(0, 0)
+        halo_start(8 + s)
+    for s in range(2, 4):
+        gather_step(s)
+        halo_start(8 + s)
+        for side in range(2):
+            gram_copy(0, side, s - 2).start()
+    gather_step(4)
+    for side in range(2):
+        gram_copy(0, side, 2).start()
     halo_grams(1)
-    gather_and_send(1, 3)
-    lax.fori_loop(6, 8, gather_rest, 0)
+    gather_and_send(1, 5)
 
     for s in range(8):
         for k in range(2):
             ring_copy(0, s, k).wait_send()
             if s < 7:
                 ring_copy(1, s, k).wait_send()
-    for b in range(BINS):
+    for n in range(12):
         for side in range(2):
-            for part in range(2):
-                for half in range(2):
-                    halo_copy(b, side, part, half).wait_send()
+            halo_copy(n, side).wait_send()
 
     tail = full[0, 128:144, :].astype(f32)
     for c in range(1, NZ):
@@ -449,7 +457,7 @@
             pltpu.VMEM((2, 16, CHAN), bf),
             dma((BINS, 2)),
             dma((2,)), dma((2,)),
-            dma((2, BINS, 2, 2)), dma((2, BINS, 2, 2)),
+            dma((2, 12)), dma((2, 12)),
             dma((2, 8, 2)), dma((2, 8, 2)),
             dma((3,)), dma((3,)),
             dma((2, 8, 2)), dma((2, 8, 2)),

time: 90.3 us -> 88.6 us (0.981)
  the two profiles are of different devices: /device:TPU:8 before, /device:TPU:16 now
where the time goes in v3:
time: 88.6 us; the launch traced here: 88.4 us
  Pallas kernels  87.8 us (99%)
    pallas_call x1, Pallas kernels, body(): pl.pallas_call(kernel, out_shape=jax.ShapeDtypeStruct((SLOTS, BINS, NBLK,...  83.7 us
    pallas_call x1, Pallas kernels, body(): pl.pallas_call(select_kernel, out_shape=(jax.ShapeDtypeStruct((BINS, NBLK...  4.04 us

profile of v3, /device:TPU:16, one launch (start us, length us, event | category | flops | bytes accessed | tf_op | source)
XLA Modules:
  0.0 88.4 jit_solution(3948989804643749514)
XLA Ops:
  0.6 83.7 %grams.1.g_hbm = bf16[14,2,4,2,128,128]{5,4,3,2,1,0:T(8,128)(2,1)} custom-call(s32[2]{0:T(128)} %refs_ref.1, bf16[2,2,512,512]{3,2,1,0:T(8,128)(2,1)} %spec_hbm.1), custom_call_target="tpu_custom_call" | custom-call | flops 5400000000 | bytes 8388608 | tf_op jit(solution)/shard_map/grams/pallas_call | solution.py:435
  84.4 4.0 %select.1 = (bf16[2,4,4,2,128,128]{5,4,3,2,1,0:T(8,128)(2,1)}, bf16[2,4,2,2,128,128]{5,4,3,2,1,0:T(8,128)(2,1)}) custom-call(s32[4,4]{1,0:T(4,128)} %pairs_ref.1, bf16[14,2,4,2,128,128]{5,4,3,2,1,0:T(8,128)(2,1)} %grams.1.g_hbm), custom_call_target="tpu_custom_call" | custom-call | bytes 6291456 | tf_op jit(solution)/shard_map/select/pallas_call | solution.py:475

commit v4 on v3

--- a/solution.py
+++ b/solution.py
@@ -36,7 +36,7 @@
 def kernel(
     refs_ref, spec_hbm, g_hbm,
     raw, white, lhs, halo, mine, ring, xsend, xrecv, full, stage, gsend, grecv,
-    psend, precv, inv_own, inv_halo, mask_ref,
+    psend, precv, inv_own, inv_halo, mask_ref, wref,
     load_sem, pow_s, pow_r, halo_s, halo_r, ring_s, ring_r, x_s, x_r, ag_s, ag_r,
     gs_s, gs_r, inv_s, inv_r, out_sem, far_sem,
 ):
@@ -251,38 +251,43 @@
         return remote(gsend.at[b, side, n], grecv.at[b, side, n], gs_s.at[b, side, n],
                       gs_r.at[b, side, n], fq, right if side == 0 else left)
 
-    def halo_grams(b):
-        for side, group in ((0, LEFT), (1, RIGHT)):
-            for n in range(b * 6, b * 6 + 6):
-                halo_copy(n, side).wait_recv()
-
-            def scale(i, _, side=side):
-                rows = pl.ds(i * 64, 64)
-                for part in range(2):
-                    v = halo[side, b, part, rows, :].astype(f32) * inv_halo[side, b, 0:1, :]
-                    halo[side, b, part, rows, :] = v.astype(bf)
-                return 0
-
-            lax.fori_loop(0, SEGS // 64, scale, 0)
-
-            def part_of(part, _, side=side, group=group):
-                half_gram(b, group, part, halo[side, b].reshape(2 * SEGS, 2 * BLK))
-                return 0
-
-            lax.fori_loop(0, 2, part_of, 0)
-            out_copy(b, group).start()
-            if side == 1:
-                for n, (la, lb) in enumerate(TO_RIGHT):
-                    gsend[b, 0, n, 0] = stage[b, RIGHT, lb, la, 0].T
-                    gsend[b, 0, n, 1] = -stage[b, RIGHT, lb, la, 1].T
-            else:
-                for n, (la, lb) in enumerate(TO_LEFT):
-                    gsend[b, 1, n, 0] = stage[b, LEFT, la - 2, lb, 0].T
-                    gsend[b, 1, n, 1] = -stage[b, LEFT, la - 2, lb, 1].T
+    def halo_grams(b, side):
+        group = RIGHT if side else LEFT
+        for n in range(b * 6, b * 6 + 6):
+            halo_copy(n, side).wait_recv()
+
+        def scale(i, _):
+            rows = pl.ds(i * 64, 64)
+            for part in range(2):
+                v = halo[side, b, part, rows, :].astype(f32) * inv_halo[side, b, 0:1, :]
+                halo[side, b, part, rows, :] = v.astype(bf)
+            return 0
+
+        lax.fori_loop(0, SEGS // 64, scale, 0)
+
+        def part_of(part, _):
+            half_gram(b, group, part, halo[side, b].reshape(2 * SEGS, 2 * BLK))
+            return 0
+
+        lax.fori_loop(0, 2, part_of, 0)
+        out_copy(b, group).start()
+        if side == 1:
+            for n, (la, lb) in enumerate(TO_RIGHT):
+                gsend[b, 0, n, 0] = stage[b, RIGHT, lb, la, 0].T
+                gsend[b, 0, n, 1] = -stage[b, RIGHT, lb, la, 1].T
+        else:
+            for n, (la, lb) in enumerate(TO_LEFT):
+                gsend[b, 1, n, 0] = stage[b, LEFT, la - 2, lb, 0].T
+                gsend[b, 1, n, 1] = -stage[b, LEFT, la - 2, lb, 1].T
 
     inv_copy(0).wait_recv()
     inv_copy(1).wait_recv()
-    halo_grams(0)
+    halo_grams(0, 0)
+    for s in range(8):
+        for k in range(2):
+            ring_copy(0, s, k).wait_send()
+            if s < 7:
+                ring_copy(1, s, k).wait_send()
 
     for c in x_copies:
         c.wait_recv()
@@ -301,68 +306,15 @@
     def gather_step(s):
         for k in range(2):
             ag_copy(0, s, k).wait_recv()
-
-            @pl.when(s < 7)
-            def _():
+            if s < 7:
                 ag_copy(0, s + 1, k).start()
                 ag_copy(1, s, k).wait_recv()
-
-            @pl.when(s < 6)
-            def _():
+            if s < 6:
                 ag_copy(1, s + 1, k).start()
-
-    def gather_and_send(b, first):
-        def step(s, _):
-            gather_step(s)
-            for side in range(2):
-                gram_copy(b, side, s - first).start()
-            return 0
-
-        lax.fori_loop(first, first + 3, step, 0)
-
-    for s in range(2):
-        gather_step(s)
-        halo_start(8 + s)
-    for s in range(2, 4):
-        gather_step(s)
-        halo_start(8 + s)
-        for side in range(2):
-            gram_copy(0, side, s - 2).start()
-    gather_step(4)
-    for side in range(2):
-        gram_copy(0, side, 2).start()
-    halo_grams(1)
-    gather_and_send(1, 5)
-
-    for s in range(8):
-        for k in range(2):
-            ring_copy(0, s, k).wait_send()
-            if s < 7:
-                ring_copy(1, s, k).wait_send()
-    for n in range(12):
-        for side in range(2):
-            halo_copy(n, side).wait_send()
-
-    tail = full[0, 128:144, :].astype(f32)
-    for c in range(1, NZ):
-        tail = tail + full[c, 128:144, :].astype(f32)
-    for b in range(BINS):
-        inv = tail[b * 3:b * 3 + 1] + tail[b * 3 + 1:b * 3 + 2] + tail[b * 3 + 2:b * 3 + 3]
-
-        def scale(i, _, b=b, inv=inv):
-            c = b * 8 + i // 2
-            rows = pl.ds(pl.multiple_of(lax.rem(i, 2) * 64, 64), 64)
-            mine[c, rows, :] = (full[c, rows, :].astype(f32) * inv).astype(bf)
-            return 0
-
-        lax.fori_loop(0, 16, scale, 0)
-
-        def part_of(part, _, b=b):
-            half_gram(b, REFS, part, mine[b * 8:b * 8 + 8].reshape(2 * SEGS, 2 * BLK))
-            return 0
-
-        lax.fori_loop(0, 2, part_of, 0)
-        out_copy(b, REFS).start()
+        if s > 0:
+            for k in range(2):
+                ag_copy(0, s - 1, k).wait_send()
+                ag_copy(1, s - 1, k).wait_send()
 
     def far_copy(b, side, n):
         if side == 0:
@@ -374,12 +326,69 @@
         return pltpu.make_async_copy(
             grecv.at[b, side, n], g_hbm.at[slot, b, a], far_sem.at[b, side, n])
 
-    for b in range(BINS):
+    def far_start(b):
         for side in range(2):
             for n in range(3):
                 gram_copy(b, side, n).wait_recv()
                 far_copy(b, side, n).start()
 
+    gather_step(0)
+    halo_start(8)
+    halo_grams(0, 1)
+    gather_step(1)
+    halo_start(9)
+    for s in range(2, 4):
+        gather_step(s)
+        halo_start(8 + s)
+        for side in range(2):
+            gram_copy(0, side, s - 2).start()
+    gather_step(4)
+    for side in range(2):
+        gram_copy(0, side, 2).start()
+    halo_grams(1, 0)
+    gather_step(5)
+    gram_copy(1, 1, 0).start()
+    gram_copy(1, 1, 1).start()
+    halo_grams(1, 1)
+    gather_step(6)
+    gram_copy(1, 1, 2).start()
+    gram_copy(1, 0, 0).start()
+    far_start(0)
+    gather_step(7)
+    gram_copy(1, 0, 1).start()
+    gram_copy(1, 0, 2).start()
+
+    tail = full[0, 128:144, :].astype(f32)
+    for c in range(1, NZ):
+        tail = tail + full[c, 128:144, :].astype(f32)
+    for b in range(BINS):
+        inv = tail[b * 3:b * 3 + 1] + tail[b * 3 + 1:b * 3 + 2] + tail[b * 3 + 2:b * 3 + 3]
+
+        def scale(i, _, b=b, inv=inv):
+            c = b * 8 + i // 2
+            rows = pl.ds(pl.multiple_of(lax.rem(i, 2) * 64, 64), 64)
+            wref[c, rows, :] = (full[c, rows, :].astype(f32) * inv).astype(bf)
+            return 0
+
+        lax.fori_loop(0, 16, scale, 0)
+
+        def part_of(part, _, b=b):
+            half_gram(b, REFS, part, wref[b * 8:b * 8 + 8].reshape(2 * SEGS, 2 * BLK))
+            return 0
+
+        lax.fori_loop(0, 2, part_of, 0)
+        out_copy(b, REFS).start()
+
+    far_start(1)
+    for n in range(12):
+        for side in range(2):
+            halo_copy(n, side).wait_send()
+    for c in x_copies:
+        c.wait_send()
+    for side in range(2):
+        inv_copy(side).wait_send()
+    for k in range(2):
+        ag_copy(0, 7, k).wait_send()
     for b in range(BINS):
         for side in range(2):
             for n in range(3):
@@ -387,21 +396,6 @@
                 far_copy(b, side, n).wait()
         for group in range(5):
             out_copy(b, group).wait()
-    for c in x_copies:
-        c.wait_send()
-    for side in range(2):
-        inv_copy(side).wait_send()
-
-    def drain(s, _):
-        for k in range(2):
-            ag_copy(0, s, k).wait_send()
-
-            @pl.when(s < 7)
-            def _():
-                ag_copy(1, s, k).wait_send()
-        return 0
-
-    lax.fori_loop(0, 8, drain, 0)
 
 
 def select_kernel(pairs_ref, g_hbm, pair_out, ref_out, pair_buf, ref_buf, pair_sem, ref_sem):
@@ -455,6 +449,7 @@
             pltpu.VMEM((BINS, 8, CHAN), jnp.float32),
             pltpu.VMEM((2, BINS, 8, 2 * BLK), jnp.float32),
             pltpu.VMEM((2, 16, CHAN), bf),
+            pltpu.VMEM((NZ, 128, 2 * BLK), bf),
             dma((BINS, 2)),
             dma((2,)), dma((2,)),
             dma((2, 12)), dma((2, 12)),

time: 88.6 us -> 88.4 us (level)
  no operation moved by 1% of the time
where the time goes in v4:
time: 88.4 us; the launch traced here: 88.2 us
  Pallas kernels  87.5 us (99%)
    pallas_call x1, Pallas kernels, body(): pl.pallas_call(kernel, out_shape=jax.ShapeDtypeStruct((SLOTS, BINS, NBLK,...  83.5 us
    pallas_call x1, Pallas kernels, body(): pl.pallas_call(select_kernel, out_shape=(jax.ShapeDtypeStruct((BINS, NBLK...  4.04 us

profile of v4, /device:TPU:16, one launch (start us, length us, event | category | flops | bytes accessed | tf_op | source)
XLA Modules:
  0.0 88.2 jit_solution(9967240717830679787)
XLA Ops:
  0.6 83.5 %grams.1.g_hbm = bf16[14,2,4,2,128,128]{5,4,3,2,1,0:T(8,128)(2,1)} custom-call(s32[2]{0:T(128)} %refs_ref.1, bf16[2,2,512,512]{3,2,1,0:T(8,128)(2,1)} %spec_hbm.1), custom_call_target="tpu_custom_call" | custom-call | flops 5400000000 | bytes 8388608 | tf_op jit(solution)/shard_map/grams/pallas_call | solution.py:429
  84.1 4.0 %select.1 = (bf16[2,4,4,2,128,128]{5,4,3,2,1,0:T(8,128)(2,1)}, bf16[2,4,2,2,128,128]{5,4,3,2,1,0:T(8,128)(2,1)}) custom-call(s32[4,4]{1,0:T(4,128)} %pairs_ref.1, bf16[14,2,4,2,128,128]{5,4,3,2,1,0:T(8,128)(2,1)} %grams.1.g_hbm), custom_call_target="tpu_custom_call" | custom-call | bytes 6291456 | tf_op jit(solution)/shard_map/select/pallas_call | solution.py:470

commit v5 on v4

--- a/solution.py
+++ b/solution.py
@@ -294,17 +294,16 @@
     full[z] = xsend[...] + xrecv[0] + xrecv[1] + xrecv[2]
 
     def ag_copy(way, s, k):
-        rows = pl.ds(0, 64) if k == 0 else pl.ds(64, 80)
         c = lax.rem(z + NZ - s, NZ) if way == 0 else lax.rem(z + s, NZ)
-        return remote(full.at[c, rows], full.at[c, rows], ag_s.at[way, s, k], ag_r.at[way, s, k],
+        return remote(full.at[c], full.at[c], ag_s.at[way, s, k], ag_r.at[way, s, k],
                       fq, z_up if way == 0 else z_dn)
 
-    for k in range(2):
+    for k in range(1):
         for way in range(2):
             ag_copy(way, 0, k).start()
 
     def gather_step(s):
-        for k in range(2):
+        for k in range(1):
             ag_copy(0, s, k).wait_recv()
             if s < 7:
                 ag_copy(0, s + 1, k).start()
@@ -312,7 +311,7 @@
             if s < 6:
                 ag_copy(1, s + 1, k).start()
         if s > 0:
-            for k in range(2):
+            for k in range(1):
                 ag_copy(0, s - 1, k).wait_send()
                 ag_copy(1, s - 1, k).wait_send()
 
@@ -387,7 +386,7 @@
         c.wait_send()
     for side in range(2):
         inv_copy(side).wait_send()
-    for k in range(2):
+    for k in range(1):
         ag_copy(0, 7, k).wait_send()
     for b in range(BINS):
         for side in range(2):

time: 88.4 us -> 90.1 us (1.019)
  Pallas kernels: 87.5 us -> 89.2 us
    pallas_call x1, Pallas kernels: 83.5 us -> 85.2 us  [body(): pl.pallas_call(kernel, out_shape=jax.ShapeDtypeStruct((SLOTS, BINS, NBLK,...]
where the time goes in v5:
time: 90.1 us; the launch traced here: 89.9 us
  Pallas kernels  89.2 us (99%)
    pallas_call x1, Pallas kernels, body(): pl.pallas_call(kernel, out_shape=jax.ShapeDtypeStruct((SLOTS, BINS, NBLK,...  85.2 us
    pallas_call x1, Pallas kernels, body(): pl.pallas_call(select_kernel, out_shape=(jax.ShapeDtypeStruct((BINS, NBLK...  4.04 us

profile of v5, /device:TPU:16, one launch (start us, length us, event | category | flops | bytes accessed | tf_op | source)
XLA Modules:
  0.0 89.9 jit_solution(12044614632829043178)
XLA Ops:
  0.6 85.2 %grams.1.g_hbm = bf16[14,2,4,2,128,128]{5,4,3,2,1,0:T(8,128)(2,1)} custom-call(s32[2]{0:T(128)} %refs_ref.1, bf16[2,2,512,512]{3,2,1,0:T(8,128)(2,1)} %spec_hbm.1), custom_call_target="tpu_custom_call" | custom-call | flops 5400000000 | bytes 8388608 | tf_op jit(solution)/shard_map/grams/pallas_call | solution.py:428
  85.8 4.0 %select.1 = (bf16[2,4,4,2,128,128]{5,4,3,2,1,0:T(8,128)(2,1)}, bf16[2,4,2,2,128,128]{5,4,3,2,1,0:T(8,128)(2,1)}) custom-call(s32[4,4]{1,0:T(4,128)} %pairs_ref.1, bf16[14,2,4,2,128,128]{5,4,3,2,1,0:T(8,128)(2,1)} %grams.1.g_hbm), custom_call_target="tpu_custom_call" | custom-call | bytes 6291456 | tf_op jit(solution)/shard_map/select/pallas_call | solution.py:469
